TPU v7x, 256 devices: a whole 4x4x8 slice. The times are simulated.
256 devices in a mesh: sub: 32 (over z, y), top: 8 (over x, core).
Axes of the slice: x: 4, y: 4, z: 8, core: 2. Of those that a mesh axis runs over, the one named last changes fastest.
Arguments:
- coords: float32 [3, 1048576], P(None, ('top', 'sub')), may hold values from 0 to 1, as said below
- vectors: float32 [1048576, 128], P(('top', 'sub')), may hold values from -6 to 6
- order: int32 [256, 4096], P(('top', 'sub')), may hold values from 0 to 4095, each once within a row
- generators: bfloat16 [1048576, 128], P(('top', 'sub')), may hold values from -0.125 to 0.125
- leaf_transfer: bfloat16 [512, 128, 128], P(('top', 'sub')), may hold values from -0.375 to 0.375
- leaf_coupling: bfloat16 [256, 128, 128], P(('top', 'sub')), may hold values from -0.5 to 0.5
- sub_transfer: bfloat16 [8, 62, 128, 128], P('top'), may hold values from -0.375 to 0.375
- sub_coupling: bfloat16 [8, 31, 128, 128], P('top'), may hold values from -0.5 to 0.5
- top_transfer: bfloat16 [12, 128, 128], replicated, may hold values from -0.375 to 0.375
- top_coupling: bfloat16 [7, 128, 128], replicated, may hold values from -0.5 to 0.5
Outputs:
- product: float32 [1048576, 128], P(('top', 'sub'))
Inputs may be any that keep to these rules, and one draw needn't show every extreme that they name: Each row of order is a permutation of 0 to 4095. `coords`: coordinates lie in the unit cube.
All inputs are finite; a program needn't handle non-finite values.
Results may differ from a plain program's by a relative error of at most 0.0035.
Values sent between devices are 32-bit elements; how exact they have to be, the bound alone decides.
A program may use at most 64 MiB of HBM per device.

v0:
```python
import jax
import jax.numpy as jnp
from jax import lax
from jax.sharding import PartitionSpec as P

PRECISE = lax.Precision.HIGHEST
NUGGET = 0.1
DECAY_RATE = 3.0**0.5 / 0.004


def swapped(value, axis, distance):
    mask = 2**distance
    pairs = [(source, source ^ mask) for source in range(lax.axis_size(axis))]
    return lax.ppermute(value, axis, pairs)


def lift_coeffs(transfer, coeffs):
    return jnp.dot(transfer.astype(jnp.float32).T, coeffs, precision=PRECISE)


def push_field(transfer, field_now):
    return jnp.dot(transfer.astype(jnp.float32), field_now, precision=PRECISE)


def couple_left(couple, coeffs):
    return jnp.dot(couple.astype(jnp.float32), coeffs, precision=PRECISE)


def couple_right(couple, coeffs):
    return jnp.dot(couple.astype(jnp.float32).T, coeffs, precision=PRECISE)


def couple_sibling(couple, sibling, is_left):
    return jnp.where(is_left, couple_left(couple, sibling), couple_right(couple, sibling))


def level_up(coeffs, transfer, couple):
    portion = jax.vmap(lift_coeffs)(transfer, coeffs)
    left_terms = jax.vmap(couple_left)(couple, coeffs[1::2])
    right_terms = jax.vmap(couple_right)(couple, coeffs[0::2])
    sibling_terms = jnp.stack([left_terms, right_terms], axis=1).reshape(coeffs.shape)
    return (portion[0::2] + portion[1::2], sibling_terms)


def leaf_coeffs(gen_rows, rounded):
    return lax.dot_general(
        gen_rows, rounded, (((0,), (0,)), ((), ())), preferred_element_type=jnp.float32
    )


def leaf_apply(packed):
    points, rounded, ordered, gen_rows, leaf_field = packed
    leaf_size = points.shape[1]
    block_size = min(512, leaf_size)
    row_points = points.reshape(3, leaf_size // block_size, block_size).transpose(1, 0, 2)

    def nearby(block_points):
        offset = block_points[:, :, None] - points[:, None, :]
        radius = jnp.sqrt(jnp.sum(offset * offset, axis=0))
        kernel = ((1.0 + DECAY_RATE * radius) * jnp.exp(-DECAY_RATE * radius)).astype(jnp.bfloat16)
        return jnp.dot(kernel, rounded, preferred_element_type=jnp.float32)

    direct = lax.map(nearby, row_points).reshape(leaf_size, rounded.shape[1])
    far_part = jnp.dot(
        gen_rows, leaf_field.astype(jnp.bfloat16), preferred_element_type=jnp.float32
    )
    return direct + far_part + NUGGET * ordered


def local(
    coords,
    vectors,
    order,
    generators,
    leaf_transfer,
    leaf_coupling,
    sub_transfer,
    sub_coupling,
    top_transfer,
    top_coupling,
):
    ordered = vectors[order[0]]
    leaf_count = leaf_transfer.shape[0]
    leaf_size = ordered.shape[0] // leaf_count
    columns = ordered.shape[1]
    rank_size = generators.shape[1]
    ordered_leaves = ordered.reshape(leaf_count, leaf_size, columns)
    rounded = ordered_leaves.astype(jnp.bfloat16)
    gen_rows = generators.reshape(leaf_count, leaf_size, rank_size)
    leaf_start = jax.vmap(leaf_coeffs)(gen_rows, rounded)
    device_coeffs, leaf_fields = level_up(leaf_start, leaf_transfer, leaf_coupling)
    coeffs = device_coeffs[0]
    sub_count = lax.axis_size("sub")
    top_count = lax.axis_size("top")
    sub_place = lax.axis_index("sub")
    top_place = lax.axis_index("top")
    transfer_rows = sub_transfer[0]
    couple_rows = sub_coupling[0]
    group_transfer = top_transfer[top_count + top_place - 4]
    own_transfer = transfer_rows[sub_count + sub_place - 2]
    down_terms = []
    heap_node = sub_count + sub_place
    for level_bit in range(sub_count.bit_length() - 1):
        portion = lift_coeffs(own_transfer, coeffs)
        sib_coeffs, sib_portion = swapped((coeffs, portion), "sub", level_bit)
        parent = heap_node // 2
        down_terms.append(
            (own_transfer, couple_sibling(couple_rows[parent - 1], sib_coeffs, heap_node % 2 == 0))
        )
        coeffs = portion + sib_portion
        heap_node = parent
        if sub_count >> level_bit + 1 > 1:
            own_transfer = transfer_rows[heap_node - 2]
        else:
            own_transfer = group_transfer
    heap_node = top_count + top_place
    levels_top = top_count.bit_length() - 1
    for level_bit in range(levels_top):
        portion = lift_coeffs(own_transfer, coeffs)
        sib_coeffs, sib_portion = swapped((coeffs, portion), "top", level_bit)
        parent = heap_node // 2
        down_terms.append(
            (own_transfer, couple_sibling(top_coupling[parent - 1], sib_coeffs, heap_node % 2 == 0))
        )
        coeffs = portion + sib_portion
        heap_node = parent
        if level_bit + 1 < levels_top:
            if top_count >> level_bit + 1 >= 4:
                own_transfer = top_transfer[heap_node - 4]
            else:
                own_transfer = jnp.zeros_like(own_transfer)
    field_now = jnp.zeros((rank_size, columns), jnp.float32)
    for transfer, incoming in reversed(down_terms):
        field_now = push_field(transfer, field_now) + incoming
    repeated = jnp.repeat(field_now[None], leaf_count, axis=0)
    leaf_field = jax.vmap(push_field)(leaf_transfer, repeated) + leaf_fields
    points = coords.reshape(3, leaf_count, leaf_size).transpose(1, 0, 2)
    nearby_rows = lax.map(leaf_apply, (points, rounded, ordered_leaves, gen_rows, leaf_field))
    flattened = nearby_rows.reshape(leaf_count * leaf_size, columns)
    return jnp.zeros_like(flattened).at[order[0]].set(flattened)


def solution(mesh):
    in_specs = (
        P(None, ("top", "sub")),
        P(("top", "sub"), None),
        P(("top", "sub"), None),
        P(("top", "sub"), None),
        P(("top", "sub"), None, None),
        P(("top", "sub"), None, None),
        P("top", None, None, None),
        P("top", None, None, None),
        P(),
        P(),
    )
    out_specs = P(("top", "sub"), None)
    return jax.shard_map(local, mesh=mesh, in_specs=in_specs, out_specs=out_specs, check_vma=False)
```

profile of v0, /device:TPU:4, one launch (start us, length us, event | category | flops | bytes accessed | tf_op | source)
XLA Modules:
  0.0 144.3 jit_solution(8411725637113821357)
XLA Ops:
  1.6 14.2 %gather_fusion = f32[4096,128]{1,0:T(8,128)} fusion(f32[4096,128]{1,0:T(8,128)S(1)} %copy-done, s32[4096]{0:T(1024)S(1)} %broadcast_clamp_fusion), kind=kCustom, calls=%fused_computation | custom fusion | bytes 4210688 | tf_op jit(solution)/shard_map/gather | solution.py:82
  15.8 2.8 %convert_element_type.9 = bf16[2,2048,128]{2,1,0:T(8,128)(2,1)} convert(f32[2,2048,128]{2,1,0:T(8,128)} %bitcast.200) | non-fusion elementwise | flops 524288 | bytes 3145728 | tf_op jit(solution)/shard_map/convert_element_type | solution.py:88
  18.6 1.7 %fusion.140 = f32[2,128,128]{2,1,0:T(8,128)S(1)} fusion(bf16[2,2048,128]{2,1,0:T(8,128)(2,1)} %convert_element_type.9, bf16[2,2048,128]{2,1,0:T(8,128)(2,1)S(1)} %bitcast.204), kind=kOutput, calls=%fused_computation.167 | convolution fusion | flops 134217728 | bytes 2228224 | tf_op jit(solution)/shard_map/vmap()/dot_general | solution.py:46
  20.6 1.7 %collective-permute-start.14 = (f32[128,128]{0,1:T(8,128)S(1)}, f32[128,128]{0,1:T(8,128)S(1)}, u32[]{:S(2)}, u32[]{:S(2)}) collective-permute-start(f32[128,128]{0,1:T(8,128)S(1)} %fusion.24), channel_id=1, source_target_pairs={{0,8},{8,0},{16,24},{24,16},{32,40},{40,32},{48,56},{56,48},{64,72... | collective-permute-start | bytes 196616 | tf_op jit(solution)/shard_map/ppermute | solution.py:14
  22.2 1.0 fusion.78
  24.2 3.4 %collective-permute-done = f32[128,128]{1,0:T(8,128)S(1)} collective-permute-done((f32[128,128]{1,0:T(8,128)S(1)}, f32[128,128]{1,0:T(8,128)S(1)}, u32[]{:S(2)}, u32[]{:S(2)}) %collective-permute-start) | collective-permute-done | bytes 65568 | tf_op jit(solution)/shard_map/ppermute | solution.py:14
  27.6 3.0 %collective-permute-start.13 = (f32[128,128]{1,0:T(8,128)S(1)}, f32[128,128]{1,0:T(8,128)S(1)}, u32[]{:S(2)}, u32[]{:S(2)}) collective-permute-start(f32[128,128]{1,0:T(8,128)S(1)} %add.225), channel_id=1, source_target_pairs={{0,16},{8,24},{16,0},{24,8},{32,48},{40,56},{48,32},{56,40},{64,80... | collective-permute-start | bytes 196616 | tf_op jit(solution)/shard_map/ppermute | solution.py:14
  30.6 1.0 fusion.74
  32.3 1.0 fusion.28
  33.3 4.1 %collective-permute-done.1 = f32[128,128]{1,0:T(8,128)S(1)} collective-permute-done((f32[128,128]{1,0:T(8,128)S(1)}, f32[128,128]{1,0:T(8,128)S(1)}, u32[]{:S(2)}, u32[]{:S(2)}) %collective-permute-start.1) | collective-permute-done | bytes 65568 | tf_op jit(solution)/shard_map/ppermute | solution.py:14
  37.5 2.0 %collective-permute-start.12 = (f32[128,128]{1,0:T(8,128)S(1)}, f32[128,128]{1,0:T(8,128)S(1)}, u32[]{:S(2)}, u32[]{:S(2)}) collective-permute-start(f32[128,128]{1,0:T(8,128)S(1)} %add.226), channel_id=1, source_target_pairs={{0,32},{8,40},{16,48},{24,56},{32,0},{40,8},{48,16},{56,24},{64,96... | collective-permute-start | bytes 196616 | tf_op jit(solution)/shard_map/ppermute | solution.py:14
  39.5 1.0 fusion.70
  40.7 1.0 fusion.31
  41.7 3.4 %collective-permute-done.2 = f32[128,128]{1,0:T(8,128)S(1)} collective-permute-done((f32[128,128]{1,0:T(8,128)S(1)}, f32[128,128]{1,0:T(8,128)S(1)}, u32[]{:S(2)}, u32[]{:S(2)}) %collective-permute-start.2) | collective-permute-done | bytes 65568 | tf_op jit(solution)/shard_map/ppermute | solution.py:14
  45.0 3.2 %collective-permute-start.11 = (f32[128,128]{1,0:T(8,128)S(1)}, f32[128,128]{1,0:T(8,128)S(1)}, u32[]{:S(2)}, u32[]{:S(2)}) collective-permute-start(f32[128,128]{1,0:T(8,128)S(1)} %add.227), channel_id=1, source_target_pairs={{0,64},{8,72},{16,80},{24,88},{32,96},{40,104},{48,112},{56,120},{... | collective-permute-start | bytes 196616 | tf_op jit(solution)/shard_map/ppermute | solution.py:14
  48.2 1.0 fusion.66
  49.3 1.0 fusion.34
  50.3 5.5 %collective-permute-done.3 = f32[128,128]{1,0:T(8,128)S(1)} collective-permute-done((f32[128,128]{1,0:T(8,128)S(1)}, f32[128,128]{1,0:T(8,128)S(1)}, u32[]{:S(2)}, u32[]{:S(2)}) %collective-permute-start.3) | collective-permute-done | bytes 65568 | tf_op jit(solution)/shard_map/ppermute | solution.py:14
  55.9 3.3 %collective-permute-start.10 = (f32[128,128]{1,0:T(8,128)S(1)}, f32[128,128]{1,0:T(8,128)S(1)}, u32[]{:S(2)}, u32[]{:S(2)}) collective-permute-start(f32[128,128]{1,0:T(8,128)S(1)} %add.228), channel_id=1, source_target_pairs={{0,128},{8,136},{16,144},{24,152},{32,160},{40,168},{48,176},{56,1... | collective-permute-start | bytes 196616 | tf_op jit(solution)/shard_map/ppermute | solution.py:14
  59.1 1.0 fusion.62
  60.1 2.9 %collective-permute-start.4 = (f32[128,128]{1,0:T(8,128)S(1)}, f32[128,128]{1,0:T(8,128)S(1)}, u32[]{:S(2)}, u32[]{:S(2)}) collective-permute-start(f32[128,128]{1,0:T(8,128)S(1)} %fusion.62), channel_id=1, source_target_pairs={{0,128},{8,136},{16,144},{24,152},{32,160},{40,168},{48,176},{56,1... | collective-permute-start | bytes 196616 | tf_op jit(solution)/shard_map/ppermute | solution.py:14
  63.0 1.0 fusion.37
  64.0 4.5 %collective-permute-done.4 = f32[128,128]{1,0:T(8,128)S(1)} collective-permute-done((f32[128,128]{1,0:T(8,128)S(1)}, f32[128,128]{1,0:T(8,128)S(1)}, u32[]{:S(2)}, u32[]{:S(2)}) %collective-permute-start.4) | collective-permute-done | bytes 65568 | tf_op jit(solution)/shard_map/ppermute | solution.py:14
  68.6 1.0 fusion.58
  70.2 1.0 fusion.40
  71.2 1.3 collective-permute-start.8
  72.5 1.0 fusion.54
  74.7 3.2 %collective-permute-done.6 = f32[128,128]{1,0:T(8,128)S(1)} collective-permute-done((f32[128,128]{1,0:T(8,128)S(1)}, f32[128,128]{1,0:T(8,128)S(1)}, u32[]{:S(2)}, u32[]{:S(2)}) %collective-permute-start.6) | collective-permute-done | bytes 65568 | tf_op jit(solution)/shard_map/ppermute | solution.py:14
  77.9 1.1 collective-permute-start.7
  79.2 4.7 %collective-permute-done.7 = f32[128,128]{1,0:T(8,128)S(1)} collective-permute-done((f32[128,128]{1,0:T(8,128)S(1)}, f32[128,128]{1,0:T(8,128)S(1)}, u32[]{:S(2)}, u32[]{:S(2)}) %collective-permute-start.7) | collective-permute-done | bytes 65568 | tf_op jit(solution)/shard_map/ppermute | solution.py:14
  85.5 0.9 fusion.56
  86.7 0.9 fusion.60
  87.6 0.9 fusion.19
  88.6 0.9 fusion.64
  89.5 0.9 fusion.18
  90.5 0.9 fusion.68
  91.4 0.9 fusion.17
  93.3 0.9 fusion.16
  94.3 0.9 fusion.76
  95.2 1.0 fusion.15
  96.6 35.4 %while.21 = (s32[]{:T(128)}, f32[2,2048,128]{2,1,0:T(8,128)}, f32[2,3,2048]{2,1,0:T(4,128)S(1)}, bf16[2,2048,128]{2,1,0:T(8,128)(2,1)}, bf16[2,2048,128]{2,1,0:T...) while((s32[]{:T(128)}, f32[2,2048,128]{2,1,0:T(8,128)}, ...), condition=%wide.region_4.5_spmd, body=%wide.region_0.4_spmd.sunk | while | flops 349962240 | bytes 16297238 | solution.py:138
  96.6 1.9 %dynamic-slice_bitcast_fusion.4 = bf16[2048,128]{1,0:T(8,128)(2,1)} fusion(bf16[2,2048,128]{2,1,0:T(8,128)(2,1)} %get-tuple-element.243, s32[]{:T(128)} %get-tuple-element.230), kind=kLoop, calls=%fused_computation.17.clone.1 | loop fusion | bytes 1048580 | tf_op jit(solution)/shard_map/while/body/jit(dynamic_index_in_dim)/squeeze | solution.py:138
  98.5 13.0 %while.22 = (s32[]{:T(128)}, f32[4,512,128]{2,1,0:T(8,128)S(1)}, f32[4,3,512]{2,1,0:T(4,128)S(1)}, f32[3,2048]{1,0:T(4,128)S(1)}, bf16[2048,128]{1,0:T(8,128)(2,1)}, /*index=5*/s32[]{:T(128)}) while((s32[]{:T(128)}, f32[4,512,128]{2,1,0:T(8,128)S(1)}, f32[4,3,512]{2,1,0:T(4,128)S(1)}, f32[3,2048]{1,0:T(4,128)S(1)}, ...), condition=%wide.region_3.3_spmd, body=%wide.region_1.2_spmd.sunk | while | flops 282066944 | bytes 11315305 | solution.py:63
  98.5 1.2 multiply_reduce_fusion.2
  99.8 2.0 %fusion.189 = f32[4,512,128]{2,1,0:T(8,128)S(1)} fusion(f32[4,512,128]{2,1,0:T(8,128)S(1)} %get-tuple-element.209, s32[]{:T(128)} %get-tuple-element.208, bf16[2048,128]{1,0:T(8,128)(2,1)S(1)} %copy-done.1, f32[512,2048]{1,0:T(8,128)S(1)} %multiply_reduce_fusion.2), kind=kOutput, calls=%fused_computation.6.clone.1 | convolution fusion | flops 273678336 | bytes 4980740 | tf_op jit(solution)/shard_map/while/body/eval_jaxpr/while/body/eval_jaxpr/dot_general | solution.py:61
  101.8 1.2 multiply_reduce_fusion.2
  103.0 2.0 %fusion.189 = f32[4,512,128]{2,1,0:T(8,128)S(1)} fusion(f32[4,512,128]{2,1,0:T(8,128)S(1)} %get-tuple-element.209, s32[]{:T(128)} %get-tuple-element.208, bf16[2048,128]{1,0:T(8,128)(2,1)S(1)} %copy-done.1, f32[512,2048]{1,0:T(8,128)S(1)} %multiply_reduce_fusion.2), kind=kOutput, calls=%fused_computation.6.clone.1 | convolution fusion | flops 273678336 | bytes 4980740 | tf_op jit(solution)/shard_map/while/body/eval_jaxpr/while/body/eval_jaxpr/dot_general | solution.py:61
  105.0 1.2 multiply_reduce_fusion.2
  106.3 2.0 %fusion.189 = f32[4,512,128]{2,1,0:T(8,128)S(1)} fusion(f32[4,512,128]{2,1,0:T(8,128)S(1)} %get-tuple-element.209, s32[]{:T(128)} %get-tuple-element.208, bf16[2048,128]{1,0:T(8,128)(2,1)S(1)} %copy-done.1, f32[512,2048]{1,0:T(8,128)S(1)} %multiply_reduce_fusion.2), kind=kOutput, calls=%fused_computation.6.clone.1 | convolution fusion | flops 273678336 | bytes 4980740 | tf_op jit(solution)/shard_map/while/body/eval_jaxpr/while/body/eval_jaxpr/dot_general | solution.py:61
  108.3 1.2 multiply_reduce_fusion.2
  109.5 2.0 %fusion.189 = f32[4,512,128]{2,1,0:T(8,128)S(1)} fusion(f32[4,512,128]{2,1,0:T(8,128)S(1)} %get-tuple-element.209, s32[]{:T(128)} %get-tuple-element.208, bf16[2048,128]{1,0:T(8,128)(2,1)S(1)} %copy-done.1, f32[512,2048]{1,0:T(8,128)S(1)} %multiply_reduce_fusion.2), kind=kOutput, calls=%fused_computation.6.clone.1 | convolution fusion | flops 273678336 | bytes 4980740 | tf_op jit(solution)/shard_map/while/body/eval_jaxpr/while/body/eval_jaxpr/dot_general | solution.py:61
  111.6 2.7 %fusion.187 = f32[2,2048,128]{2,1,0:T(8,128)} fusion(f32[2,2048,128]{2,1,0:T(8,128)} %get-tuple-element.231, s32[]{:T(128)} %get-tuple-element.230, f32[2048,128]{1,0:T(8,128)S(1)} %bitcast.202, f32[2,2048,128]{2,1,0:T(8,128)} %get-tuple-element.246, bf16[2,2048,128]{2,1,0:T(8,128)(2,1)} %get-tuple-element.244, bf16[1,128,128]{2,1,0:T(8,128)(2,1)S(1)} %copy.21), kind=kOutput, calls=%fused_computation.14.clone.1 | convolution fusion | flops 67895296 | bytes 3703808 | tf_op jit(solution)/shard_map/while/body/eval_jaxpr/dot_general | solution.py:64
  114.3 1.9 %dynamic-slice_bitcast_fusion.4 = bf16[2048,128]{1,0:T(8,128)(2,1)} fusion(bf16[2,2048,128]{2,1,0:T(8,128)(2,1)} %get-tuple-element.243, s32[]{:T(128)} %get-tuple-element.230), kind=kLoop, calls=%fused_computation.17.clone.1 | loop fusion | bytes 1048580 | tf_op jit(solution)/shard_map/while/body/jit(dynamic_index_in_dim)/squeeze | solution.py:138
  116.2 13.0 %while.22 = (s32[]{:T(128)}, f32[4,512,128]{2,1,0:T(8,128)S(1)}, f32[4,3,512]{2,1,0:T(4,128)S(1)}, f32[3,2048]{1,0:T(4,128)S(1)}, bf16[2048,128]{1,0:T(8,128)(2,1)}, /*index=5*/s32[]{:T(128)}) while((s32[]{:T(128)}, f32[4,512,128]{2,1,0:T(8,128)S(1)}, f32[4,3,512]{2,1,0:T(4,128)S(1)}, f32[3,2048]{1,0:T(4,128)S(1)}, ...), condition=%wide.region_3.3_spmd, body=%wide.region_1.2_spmd.sunk | while | flops 282066944 | bytes 11315305 | solution.py:63
  116.2 1.2 multiply_reduce_fusion.2
  117.4 2.0 %fusion.189 = f32[4,512,128]{2,1,0:T(8,128)S(1)} fusion(f32[4,512,128]{2,1,0:T(8,128)S(1)} %get-tuple-element.209, s32[]{:T(128)} %get-tuple-element.208, bf16[2048,128]{1,0:T(8,128)(2,1)S(1)} %copy-done.1, f32[512,2048]{1,0:T(8,128)S(1)} %multiply_reduce_fusion.2), kind=kOutput, calls=%fused_computation.6.clone.1 | convolution fusion | flops 273678336 | bytes 4980740 | tf_op jit(solution)/shard_map/while/body/eval_jaxpr/while/body/eval_jaxpr/dot_general | solution.py:61
  119.4 1.2 multiply_reduce_fusion.2
  120.7 2.0 %fusion.189 = f32[4,512,128]{2,1,0:T(8,128)S(1)} fusion(f32[4,512,128]{2,1,0:T(8,128)S(1)} %get-tuple-element.209, s32[]{:T(128)} %get-tuple-element.208, bf16[2048,128]{1,0:T(8,128)(2,1)S(1)} %copy-done.1, f32[512,2048]{1,0:T(8,128)S(1)} %multiply_reduce_fusion.2), kind=kOutput, calls=%fused_computation.6.clone.1 | convolution fusion | flops 273678336 | bytes 4980740 | tf_op jit(solution)/shard_map/while/body/eval_jaxpr/while/body/eval_jaxpr/dot_general | solution.py:61
  122.7 1.2 multiply_reduce_fusion.2
  123.9 2.0 %fusion.189 = f32[4,512,128]{2,1,0:T(8,128)S(1)} fusion(f32[4,512,128]{2,1,0:T(8,128)S(1)} %get-tuple-element.209, s32[]{:T(128)} %get-tuple-element.208, bf16[2048,128]{1,0:T(8,128)(2,1)S(1)} %copy-done.1, f32[512,2048]{1,0:T(8,128)S(1)} %multiply_reduce_fusion.2), kind=kOutput, calls=%fused_computation.6.clone.1 | convolution fusion | flops 273678336 | bytes 4980740 | tf_op jit(solution)/shard_map/while/body/eval_jaxpr/while/body/eval_jaxpr/dot_general | solution.py:61
  125.9 1.2 multiply_reduce_fusion.2
  127.2 2.0 %fusion.189 = f32[4,512,128]{2,1,0:T(8,128)S(1)} fusion(f32[4,512,128]{2,1,0:T(8,128)S(1)} %get-tuple-element.209, s32[]{:T(128)} %get-tuple-element.208, bf16[2048,128]{1,0:T(8,128)(2,1)S(1)} %copy-done.1, f32[512,2048]{1,0:T(8,128)S(1)} %multiply_reduce_fusion.2), kind=kOutput, calls=%fused_computation.6.clone.1 | convolution fusion | flops 273678336 | bytes 4980740 | tf_op jit(solution)/shard_map/while/body/eval_jaxpr/while/body/eval_jaxpr/dot_general | solution.py:61
  129.3 2.7 %fusion.187 = f32[2,2048,128]{2,1,0:T(8,128)} fusion(f32[2,2048,128]{2,1,0:T(8,128)} %get-tuple-element.231, s32[]{:T(128)} %get-tuple-element.230, f32[2048,128]{1,0:T(8,128)S(1)} %bitcast.202, f32[2,2048,128]{2,1,0:T(8,128)} %get-tuple-element.246, bf16[2,2048,128]{2,1,0:T(8,128)(2,1)} %get-tuple-element.244, bf16[1,128,128]{2,1,0:T(8,128)(2,1)S(1)} %copy.21), kind=kOutput, calls=%fused_computation.14.clone.1 | convolution fusion | flops 67895296 | bytes 3703808 | tf_op jit(solution)/shard_map/while/body/eval_jaxpr/dot_general | solution.py:64
  132.0 12.3 %scatter_custom_fusion = f32[4096,128]{1,0:T(8,128)} fusion(s32[4096]{0:T(1024)S(1)} %bitcast.210, f32[4096,128]{1,0:T(8,128)} %bitcast.211, f32[]{:T(128)} %constant.201.clone.1), kind=kCustom, calls=%fused_computation.43 | custom fusion | bytes 2097664 | tf_op jit(solution)/shard_map/scatter | solution.py:140
  (85 shorter events, 9.3 us)
Async XLA Ops:
  0.0 1.6 %copy-start = (f32[4096,128]{1,0:T(8,128)S(1)}, f32[4096,128]{1,0:T(8,128)}, u32[]{:S(2)}) copy-start(f32[4096,128]{1,0:T(8,128)} %param.15) | copy-start | bytes 6291460
  15.8 2.8 %copy-start.2 = (bf16[4096,128]{1,0:T(8,128)(2,1)S(1)}, bf16[4096,128]{1,0:T(8,128)(2,1)}, u32[]{:S(2)}) copy-start(bf16[4096,128]{1,0:T(8,128)(2,1)} %param.17) | copy-start | bytes 3145732
  15.8 4.5 %copy-start.4 = (bf16[2,128,128]{2,1,0:T(8,128)(2,1)S(1)}, bf16[2,128,128]{2,1,0:T(8,128)(2,1)}, u32[]{:S(2)}) copy-start(bf16[2,128,128]{2,1,0:T(8,128)(2,1)} %param.18) | copy-start | bytes 196612
  18.6 5.2 %copy-start.6 = (bf16[1,128,128]{2,1,0:T(8,128)(2,1)S(1)}, bf16[1,128,128]{2,1,0:T(8,128)(2,1)}, u32[]{:S(2)}) copy-start(bf16[1,128,128]{2,1,0:T(8,128)(2,1)} %param.19) | copy-start | bytes 98308
  20.5 53.9 %copy-start.5 = (bf16[7,128,128]{2,1,0:T(8,128)(2,1)S(1)}, bf16[7,128,128]{2,1,0:T(8,128)(2,1)}, u32[]{:S(2)}) copy-start(bf16[7,128,128]{2,1,0:T(8,128)(2,1)} %param.23) | copy-start | bytes 688132
  20.6 11.7 %collective-permute-start.14 = (f32[128,128]{0,1:T(8,128)S(1)}, f32[128,128]{0,1:T(8,128)S(1)}, u32[]{:S(2)}, u32[]{:S(2)}) collective-permute-start(f32[128,128]{0,1:T(8,128)S(1)} %fusion.24), channel_id=1, source_target_pairs={{0,8},{8,0},{16,24},{24,16},{32,40},{40,32},{48,56},{56,48},{64,72... | collective-permute-start | bytes 196616 | tf_op jit(solution)/shard_map/ppermute | solution.py:14
  23.2 4.4 %collective-permute-start = (f32[128,128]{1,0:T(8,128)S(1)}, f32[128,128]{1,0:T(8,128)S(1)}, u32[]{:S(2)}, u32[]{:S(2)}) collective-permute-start(f32[128,128]{1,0:T(8,128)S(1)} %fusion.78), channel_id=1, source_target_pairs={{0,8},{8,0},{16,24},{24,16},{32,40},{40,32},{48,56},{56,48},{64,72... | collective-permute-start | bytes 196616 | tf_op jit(solution)/shard_map/ppermute | solution.py:14
  27.6 13.1 %collective-permute-start.13 = (f32[128,128]{1,0:T(8,128)S(1)}, f32[128,128]{1,0:T(8,128)S(1)}, u32[]{:S(2)}, u32[]{:S(2)}) collective-permute-start(f32[128,128]{1,0:T(8,128)S(1)} %add.225), channel_id=1, source_target_pairs={{0,16},{8,24},{16,0},{24,8},{32,48},{40,56},{48,32},{56,40},{64,80... | collective-permute-start | bytes 196616 | tf_op jit(solution)/shard_map/ppermute | solution.py:14
  31.6 5.9 %collective-permute-start.1 = (f32[128,128]{1,0:T(8,128)S(1)}, f32[128,128]{1,0:T(8,128)S(1)}, u32[]{:S(2)}, u32[]{:S(2)}) collective-permute-start(f32[128,128]{1,0:T(8,128)S(1)} %fusion.74), channel_id=1, source_target_pairs={{0,16},{8,24},{16,0},{24,8},{32,48},{40,56},{48,32},{56,40},{64,80... | collective-permute-start | bytes 196616 | tf_op jit(solution)/shard_map/ppermute | solution.py:14
  37.5 11.8 %collective-permute-start.12 = (f32[128,128]{1,0:T(8,128)S(1)}, f32[128,128]{1,0:T(8,128)S(1)}, u32[]{:S(2)}, u32[]{:S(2)}) collective-permute-start(f32[128,128]{1,0:T(8,128)S(1)} %add.226), channel_id=1, source_target_pairs={{0,32},{8,40},{16,48},{24,56},{32,0},{40,8},{48,16},{56,24},{64,96... | collective-permute-start | bytes 196616 | tf_op jit(solution)/shard_map/ppermute | solution.py:14
  40.5 4.6 %collective-permute-start.2 = (f32[128,128]{1,0:T(8,128)S(1)}, f32[128,128]{1,0:T(8,128)S(1)}, u32[]{:S(2)}, u32[]{:S(2)}) collective-permute-start(f32[128,128]{1,0:T(8,128)S(1)} %fusion.70), channel_id=1, source_target_pairs={{0,32},{8,40},{16,48},{24,56},{32,0},{40,8},{48,16},{56,24},{64,96... | collective-permute-start | bytes 196616 | tf_op jit(solution)/shard_map/ppermute | solution.py:14
  45.0 17.9 %collective-permute-start.11 = (f32[128,128]{1,0:T(8,128)S(1)}, f32[128,128]{1,0:T(8,128)S(1)}, u32[]{:S(2)}, u32[]{:S(2)}) collective-permute-start(f32[128,128]{1,0:T(8,128)S(1)} %add.227), channel_id=1, source_target_pairs={{0,64},{8,72},{16,80},{24,88},{32,96},{40,104},{48,112},{56,120},{... | collective-permute-start | bytes 196616 | tf_op jit(solution)/shard_map/ppermute | solution.py:14
  49.2 6.7 %collective-permute-start.3 = (f32[128,128]{1,0:T(8,128)S(1)}, f32[128,128]{1,0:T(8,128)S(1)}, u32[]{:S(2)}, u32[]{:S(2)}) collective-permute-start(f32[128,128]{1,0:T(8,128)S(1)} %fusion.66), channel_id=1, source_target_pairs={{0,64},{8,72},{16,80},{24,88},{32,96},{40,104},{48,112},{56,120},{... | collective-permute-start | bytes 196616 | tf_op jit(solution)/shard_map/ppermute | solution.py:14
  55.9 14.4 %collective-permute-start.10 = (f32[128,128]{1,0:T(8,128)S(1)}, f32[128,128]{1,0:T(8,128)S(1)}, u32[]{:S(2)}, u32[]{:S(2)}) collective-permute-start(f32[128,128]{1,0:T(8,128)S(1)} %add.228), channel_id=1, source_target_pairs={{0,128},{8,136},{16,144},{24,152},{32,160},{40,168},{48,176},{56,1... | collective-permute-start | bytes 196616 | tf_op jit(solution)/shard_map/ppermute | solution.py:14
  60.1 8.4 %collective-permute-start.4 = (f32[128,128]{1,0:T(8,128)S(1)}, f32[128,128]{1,0:T(8,128)S(1)}, u32[]{:S(2)}, u32[]{:S(2)}) collective-permute-start(f32[128,128]{1,0:T(8,128)S(1)} %fusion.62), channel_id=1, source_target_pairs={{0,128},{8,136},{16,144},{24,152},{32,160},{40,168},{48,176},{56,1... | collective-permute-start | bytes 196616 | tf_op jit(solution)/shard_map/ppermute | solution.py:14
  68.5 5.9 %collective-permute-start.9 = (f32[128,128]{1,0:T(8,128)S(1)}, f32[128,128]{1,0:T(8,128)S(1)}, u32[]{:S(2)}, u32[]{:S(2)}) collective-permute-start(f32[128,128]{1,0:T(8,128)S(1)} %add.229), channel_id=1, source_target_pairs={{0,1},{1,0},{2,3},{3,2},{4,5},{5,4},{6,7},{7,6},{8,9},{9,8},{10,11... | collective-permute-start | bytes 196616 | tf_op jit(solution)/shard_map/ppermute | solution.py:14
  69.6 1.6 %collective-permute-start.5 = (f32[128,128]{1,0:T(8,128)S(1)}, f32[128,128]{1,0:T(8,128)S(1)}, u32[]{:S(2)}, u32[]{:S(2)}) collective-permute-start(f32[128,128]{1,0:T(8,128)S(1)} %fusion.58), channel_id=1, source_target_pairs={{0,1},{1,0},{2,3},{3,2},{4,5},{5,4},{6,7},{7,6},{8,9},{9,8},{10,11... | collective-permute-start | bytes 196616 | tf_op jit(solution)/shard_map/ppermute | solution.py:14
  71.2 7.7 %collective-permute-start.8 = (f32[128,128]{1,0:T(8,128)S(1)}, f32[128,128]{1,0:T(8,128)S(1)}, u32[]{:S(2)}, u32[]{:S(2)}) collective-permute-start(f32[128,128]{1,0:T(8,128)S(1)} %add.230), channel_id=1, source_target_pairs={{0,2},{1,3},{2,0},{3,1},{4,6},{5,7},{6,4},{7,5},{8,10},{9,11},{10,... | collective-permute-start | bytes 196616 | tf_op jit(solution)/shard_map/ppermute | solution.py:14
  73.5 4.4 %collective-permute-start.6 = (f32[128,128]{1,0:T(8,128)S(1)}, f32[128,128]{1,0:T(8,128)S(1)}, u32[]{:S(2)}, u32[]{:S(2)}) collective-permute-start(f32[128,128]{1,0:T(8,128)S(1)} %fusion.54), channel_id=1, source_target_pairs={{0,2},{1,3},{2,0},{3,1},{4,6},{5,7},{6,4},{7,5},{8,10},{9,11},{10,... | collective-permute-start | bytes 196616 | tf_op jit(solution)/shard_map/ppermute | solution.py:14
  77.9 18.7 %copy-start.3 = (f32[3,4096]{1,0:T(4,128)S(1)}, f32[3,4096]{1,0:T(4,128)}, u32[]{:S(2)}) copy-start(f32[3,4096]{1,0:T(4,128)} %param.14) | copy-start | bytes 147460
  77.9 6.0 %collective-permute-start.7 = (f32[128,128]{1,0:T(8,128)S(1)}, f32[128,128]{1,0:T(8,128)S(1)}, u32[]{:S(2)}, u32[]{:S(2)}) collective-permute-start(f32[128,128]{1,0:T(8,128)S(1)} %add.231), channel_id=1, source_target_pairs={{0,4},{1,5},{2,6},{3,7},{4,0},{5,1},{6,2},{7,3},{8,12},{9,13},{10,... | collective-permute-start | bytes 196616 | tf_op jit(solution)/shard_map/ppermute | solution.py:14
  98.5 1.2 copy-start.1
  101.8 1.3 copy-start.1
  105.0 1.3 copy-start.1
  108.3 1.3 copy-start.1
  116.2 1.2 copy-start.1
  119.4 1.3 copy-start.1
  122.7 1.3 copy-start.1
  125.9 1.3 copy-start.1
where the time goes:
time: 146 us; the launch traced here: 144 us
  matrix products  48.1 us (33%)
  local copies, waits for them, and re-layouts  31.4 us (22%)
  waiting for transfers between devices  28.9 us (20%)
  starting transfers between devices  21.4 us (15%)
  other arithmetic  13.6 us (9%)
    ppermute x15, waiting for transfers between devices, swapped(): return lax.ppermute(value, axis, pairs)  28.9 us
    ppermute x15, starting transfers between devices, swapped(): return lax.ppermute(value, axis, pairs)  21.4 us
    dot_general x8, matrix products, nearby(): return jnp.dot(kernel, rounded, preferred_element_type=jnp.float32)  15.6 us
    gather x1, local copies, waits for them, and re-layouts, local(): ordered = vectors[order[0]]  14.2 us
    scatter x1, local copies, waits for them, and re-layouts, local(): return jnp.zeros_like(flattened).at[order[0]].set(flattened)  12.3 us
    reduce_sum x8, other arithmetic, nearby(): radius = jnp.sqrt(jnp.sum(offset * offset, axis=0))  9.88 us
    dot_general x8, matrix products, lift_coeffs(): return jnp.dot(transfer.astype(jnp.float32).T, coeffs, precision=PRECISE)  7.13 us
    dot_general x8, matrix products, push_field(): return jnp.dot(transfer.astype(jnp.float32), field_now, precision=PRECISE)  6.87 us
  transfers between devices with their start and end apart: 15, of which 7 were waited for; matrix products, arithmetic and copies ran while one was open for 9% of the time, Pallas kernels for 0%

commit v1 on v0

v1 whole, which is shorter than its diff:
```python
import functools

import jax
import jax.numpy as jnp
from jax import lax
from jax.experimental import pallas as pl
from jax.experimental.pallas import tpu as pltpu
from jax.sharding import PartitionSpec as P

NUGGET = 0.1
DECAY_RATE = 3.0**0.5 / 0.004
TINY = 1e-30
BLOCK = 256
BLOCKS = 8
WIDE = 5 * BLOCK
NARROW = 4 * BLOCK
F32 = jnp.float32
BF16 = jnp.bfloat16
NN = (((1,), (0,)), ((), ()))
NT = (((1,), (1,)), ((), ()))


def pieces(x):
    high = x.astype(BF16)
    low = (x - high.astype(F32)).astype(BF16)
    return jnp.concatenate([high, low], axis=0)


def product(x, matrix, form):
    rows = x.shape[0]
    both = lax.dot_general(pieces(x), matrix, form, preferred_element_type=F32)
    return both[:rows] + both[rows:]


def main_kernel(
    n_sub,
    n_top,
    order_ref,
    coords_ref,
    vectors_hbm,
    gen_hbm,
    leaf_w_hbm,
    leaf_b_hbm,
    sub_w_hbm,
    sub_b_hbm,
    top_w_hbm,
    top_b_hbm,
    y_hbm,
    vec,
    ordered,
    v_ext,
    v_t,
    gen,
    leaf_w,
    leaf_b,
    sub_w,
    sub_b,
    top_w,
    top_b,
    x_rows,
    x_cols,
    k_buf,
    y_row,
    y_col,
    send_c,
    coef,
    sib,
    field,
    send_f,
    back,
    top_c,
    dev_f,
    g_leaf,
    y_out,
    in_sem,
    out_sem,
    own_sem,
    send_sem,
    recv_sem,
):
    leaf = v_t.shape[2]
    rows = vec.shape[0]
    width = vec.shape[1]
    share = width // n_sub
    me_sub = lax.axis_index("sub")
    me_top = lax.axis_index("top")

    barrier = pltpu.get_barrier_semaphore()

    def greet(axis, count, place):
        def one(k, _):
            pl.semaphore_signal(
                barrier,
                inc=1,
                device_id={axis: lax.rem(place + k, count)},
                device_id_type=pl.DeviceIdType.MESH,
            )
            return 0

        lax.fori_loop(1, count, one, 0)

    loads = [
        pltpu.make_async_copy(source, target, in_sem.at[i])
        for i, (source, target) in enumerate(
            [
                (vectors_hbm, vec),
                (gen_hbm, gen),
                (leaf_w_hbm, leaf_w),
                (leaf_b_hbm, leaf_b),
                (sub_w_hbm, sub_w),
                (sub_b_hbm, sub_b),
                (top_w_hbm, top_w),
                (top_b_hbm, top_b),
            ]
        )
    ]
    for load in loads:
        load.start()
    greet("sub", n_sub, me_sub)
    greet("top", n_top, me_top)

    def spread(block, _):
        start = pl.multiple_of(block * 128, 128)
        for axis in range(3):
            row = coords_ref[axis : axis + 1, pl.ds(start, 128)] * DECAY_RATE
            x_rows[axis, pl.ds(start, 128), :] = jnp.broadcast_to(row, (128, 128)).T
        return 0

    lax.fori_loop(0, rows // 128, spread, 0)
    extra = v_ext.shape[1] - leaf
    for at in range(2):
        for axis in range(3):
            row = coords_ref[axis : axis + 1, at * leaf : (at + 1) * leaf] * DECAY_RATE
            whole = jnp.broadcast_to(row, (8, leaf))
            x_cols[axis, at, :, :leaf] = whole
            x_cols[axis, at, :, leaf:] = whole[:, :extra]
    y_col[...] = jnp.zeros_like(y_col)

    loads[0].wait()

    def move(group, _):
        base = pl.multiple_of(group * 16, 16)
        for k in range(16):
            ordered[pl.ds(base + k, 1), :] = vec[pl.ds(order_ref[0, base + k], 1), :]
        return 0

    lax.fori_loop(0, rows // 16, move, 0)
    for at in range(2):

        def turn(block, _):
            start = pl.multiple_of(block * 128, 128)
            part = ordered[pl.ds(at * leaf + start, 128), :]
            v_ext[at, pl.ds(start, 128), :] = part.astype(BF16)
            v_t[at, :, pl.ds(start, 128)] = part.T.astype(BF16)
            return 0

        lax.fori_loop(0, leaf // 128, turn, 0)
        v_ext[at, leaf:, :] = v_ext[at, :extra, :]

    for load in loads[1:4]:
        load.wait()
    left = jnp.dot(v_t[0], gen[:leaf, :], preferred_element_type=F32)
    right = jnp.dot(v_t[1], gen[leaf:, :], preferred_element_type=F32)
    device_c = product(left, leaf_w[0], NN) + product(right, leaf_w[1], NN)
    for r in range(n_sub):
        send_c[r] = device_c[r * share : (r + 1) * share, :]
    pl.semaphore_wait(barrier, n_sub + n_top - 2)

    def exchange(axis, count, place, stage, source, target, base):
        def copy(partner, slot):
            return pltpu.make_async_remote_copy(
                src_ref=source(partner),
                dst_ref=target.at[base + slot],
                send_sem=send_sem.at[stage, partner],
                recv_sem=recv_sem.at[stage, slot],
                device_id={axis: partner},
                device_id_type=pl.DeviceIdType.MESH,
            )

        def start(k, _):
            copy(lax.rem(place + k, count), place).start()
            return 0

        def finish_send(k, _):
            copy(lax.rem(place + k, count), place).wait_send()
            return 0

        def finish_recv(k, _):
            partner = lax.rem(place + k, count)
            copy(partner, partner).wait_recv()
            return 0

        return (
            lambda: lax.fori_loop(1, count, start, 0),
            lambda: lax.fori_loop(1, count, finish_send, 0),
            lambda: lax.fori_loop(1, count, finish_recv, 0),
        )

    up_start, up_sent, up_here = exchange(
        "sub", n_sub, me_sub, 0, lambda partner: send_c.at[partner], coef, n_sub
    )
    up_start()
    coef[n_sub + me_sub] = send_c[me_sub]
    g_leaf[0] = product(right, leaf_b[0], NT)
    g_leaf[1] = product(left, leaf_b[0], NN)

    def evaluate(at, block, size):
        def some_rows(part, _):
            first = part * 32
            here = pl.ds(pl.multiple_of(at * leaf + block * BLOCK + first, 32), 32)
            x_i = [x_rows[axis, here, :] for axis in range(3)]
            x_i = [jnp.concatenate([x, x], axis=1) for x in x_i]
            for step in range(size // BLOCK):
                there = pl.ds(pl.multiple_of((block + step) * BLOCK, BLOCK), BLOCK)
                total = None
                for axis in range(3):
                    x_j = x_cols[axis, at, :, there]
                    offset = x_i[axis] - jnp.concatenate([x_j] * 4, axis=0)
                    square = offset * offset
                    total = square + TINY if total is None else total + square
                scaled = total * lax.rsqrt(total)
                value = (1.0 + scaled) * jnp.exp(-scaled)
                k_buf[at, pl.ds(first, 32), pl.ds(step * BLOCK, BLOCK)] = value.astype(BF16)
            return 0

        lax.fori_loop(0, BLOCK // 32, some_rows, 0, unroll=True)

    def apply(at, block, size):
        start = pl.multiple_of(block * BLOCK, BLOCK)
        after = pl.multiple_of((block + 1) * BLOCK, BLOCK)
        y_row[at, pl.ds(start, BLOCK), :] = jnp.dot(
            k_buf[at, :, :size], v_ext[at, pl.ds(start, size), :], preferred_element_type=F32
        )
        y_col[at, :, pl.ds(after, size - BLOCK)] += jnp.dot(
            v_t[at, :, pl.ds(start, BLOCK)], k_buf[at, :, BLOCK:size], preferred_element_type=F32
        )

    def near(first, last, size):
        evaluate(0, first, size)
        apply(0, first, size)
        evaluate(1, first, size)

        def step(block, _):
            evaluate(0, block, size)
            apply(1, block - 1, size)
            evaluate(1, block, size)
            apply(0, block, size)
            return 0

        lax.fori_loop(first + 1, last, step, 0)
        apply(1, last - 1, size)

    near(0, 2, WIDE)

    loads[4].wait()
    loads[5].wait()
    up_here()

    def upward(held, matrices, parent, offset):
        pair = jnp.concatenate([held[2 * parent], held[2 * parent + 1]], axis=1)
        both = matrices[pl.ds(2 * parent - offset, 2)].reshape(2 * width, width)
        held[parent] = product(pair, both, NN)

    count = n_sub // 2
    while count >= 1:
        lax.fori_loop(
            count, 2 * count, lambda p, _: (upward(coef, sub_w, p, 2), 0)[1], 0, unroll=True
        )
        count //= 2
    top_start, top_sent, top_here = exchange(
        "top", n_top, me_top, 1, lambda partner: coef.at[1], top_c, n_top
    )
    top_start()
    top_c[n_top + me_top] = coef[1]

    def siblings(parent, _):
        matrix = sub_b[parent - 1]
        sib[2 * parent] = product(coef[2 * parent + 1], matrix, NT)
        sib[2 * parent + 1] = product(coef[2 * parent], matrix, NN)
        return 0

    lax.fori_loop(1, n_sub, siblings, 0, unroll=True)

    near(2, 4, WIDE)

    loads[6].wait()
    loads[7].wait()
    top_here()
    count = n_top // 2
    while count >= 2:
        lax.fori_loop(
            count, 2 * count, lambda p, _: (upward(top_c, top_w, p, 4), 0)[1], 0, unroll=True
        )
        count //= 2
    now = None
    count = 2
    while count <= n_top:
        node = count + me_top // (n_top // count)
        parent = node // 2
        is_left = node - 2 * parent == 0
        other = jnp.where(is_left, node + 1, node - 1)
        matrix = top_b[parent - 1]
        incoming = jnp.where(
            is_left, product(top_c[other], matrix, NT), product(top_c[other], matrix, NN)
        )
        now = incoming if now is None else product(now, top_w[node - 4], NT) + incoming
        count *= 2
    field[1] = now

    def downward(parent, _):
        both = sub_w[pl.ds(2 * parent - 2, 2)].reshape(2 * width, width)
        down = product(field[parent], both, NT)
        field[2 * parent] = down[:, :width] + sib[2 * parent]
        field[2 * parent + 1] = down[:, width:] + sib[2 * parent + 1]
        return 0

    count = 1
    while count < n_sub:
        lax.fori_loop(count, 2 * count, downward, 0, unroll=True)
        count *= 2
    down_start, down_sent, down_here = exchange(
        "sub", n_sub, me_sub, 2, lambda partner: field.at[n_sub + partner], back, 0
    )
    down_start()
    back[me_sub] = field[n_sub + me_sub]

    near(4, 8, NARROW)

    down_here()
    for r in range(n_sub):
        dev_f[r * share : (r + 1) * share, :] = back[r]
    device_f = dev_f[...]
    leaf_f = [
        (product(device_f, leaf_w[at], NT) + g_leaf[at]).astype(BF16) for at in range(2)
    ]

    writes = []
    for at in range(2):
        for block in range(BLOCKS):
            start = at * leaf + block * BLOCK
            here = slice(block * BLOCK, (block + 1) * BLOCK)
            turned = y_col[at, :, here]
            if (block + 1) * BLOCK <= extra:
                turned = turned + y_col[at, :, leaf + block * BLOCK : leaf + (block + 1) * BLOCK]
            far = lax.dot_general(
                gen[start : start + BLOCK, :], leaf_f[at], NT, preferred_element_type=F32
            )
            y_out[start : start + BLOCK, :] = (
                y_row[at, here, :] + turned.T + far + NUGGET * ordered[start : start + BLOCK, :]
            )
        half = pl.ds(at * leaf, leaf)
        write = pltpu.make_async_copy(y_out.at[half], y_hbm.at[half], out_sem.at[at])
        write.start()
        writes.append(write)
    up_sent()
    top_sent()
    down_sent()
    for write in writes:
        write.wait()


def scatter_kernel(order_ref, y_ref, out_ref):
    chunk = y_ref.shape[0]
    first = pl.program_id(0) * chunk

    def move(group, _):
        base = pl.multiple_of(group * 16, 16)
        for k in range(16):
            out_ref[pl.ds(order_ref[0, first + base + k], 1), :] = y_ref[pl.ds(base + k, 1), :]
        return 0

    lax.fori_loop(0, chunk // 16, move, 0)


def local(
    n_sub,
    n_top,
    coords,
    vectors,
    order,
    generators,
    leaf_transfer,
    leaf_coupling,
    sub_transfer,
    sub_coupling,
    top_transfer,
    top_coupling,
):
    rows, width = vectors.shape
    leaf = rows // 2
    rank = generators.shape[1]
    share = width // n_sub
    extended = leaf + 3 * BLOCK
    smem = pl.BlockSpec(memory_space=pltpu.SMEM)
    vmem = pl.BlockSpec(memory_space=pltpu.VMEM)
    hbm = pl.BlockSpec(memory_space=pl.ANY)
    scratch = [
        pltpu.VMEM((rows, width), F32),
        pltpu.VMEM((rows, width), F32),
        pltpu.VMEM((2, extended, width), BF16),
        pltpu.VMEM((2, width, leaf), BF16),
        pltpu.VMEM((rows, rank), BF16),
        pltpu.VMEM(leaf_transfer.shape, BF16),
        pltpu.VMEM(leaf_coupling.shape, BF16),
        pltpu.VMEM(sub_transfer.shape[1:], BF16),
        pltpu.VMEM(sub_coupling.shape[1:], BF16),
        pltpu.VMEM(top_transfer.shape, BF16),
        pltpu.VMEM(top_coupling.shape, BF16),
        pltpu.VMEM((3, rows, 128), F32),
        pltpu.VMEM((3, 2, 8, extended), F32),
        pltpu.VMEM((2, BLOCK, WIDE), BF16),
        pltpu.VMEM((2, leaf, width), F32),
        pltpu.VMEM((2, width, extended), F32),
        pltpu.VMEM((n_sub, share, rank), F32),
        pltpu.VMEM((2 * n_sub, share, rank), F32),
        pltpu.VMEM((2 * n_sub, share, rank), F32),
        pltpu.VMEM((2 * n_sub, share, rank), F32),
        pltpu.VMEM((n_sub, share, rank), F32),
        pltpu.VMEM((n_sub, share, rank), F32),
        pltpu.VMEM((2 * n_top, share, rank), F32),
        pltpu.VMEM((width, rank), F32),
        pltpu.VMEM((2, width, rank), F32),
        pltpu.VMEM((rows, width), F32),
        pltpu.SemaphoreType.DMA((8,)),
        pltpu.SemaphoreType.DMA((2,)),
        pltpu.SemaphoreType.DMA,
        pltpu.SemaphoreType.DMA((3, max(n_sub, n_top))),
        pltpu.SemaphoreType.DMA((3, max(n_sub, n_top))),
    ]
    y = pl.pallas_call(
        functools.partial(main_kernel, n_sub, n_top),
        out_shape=jax.ShapeDtypeStruct((rows, width), F32),
        in_specs=[smem, vmem] + [hbm] * 8,
        out_specs=hbm,
        scratch_shapes=scratch,
        compiler_params=pltpu.CompilerParams(
            collective_id=0, has_side_effects=True, vmem_limit_bytes=48 * 1024 * 1024
        ),
        name="hss_main",
    )(
        order,
        coords,
        vectors,
        generators,
        leaf_transfer,
        leaf_coupling,
        sub_transfer[0],
        sub_coupling[0],
        top_transfer,
        top_coupling,
    )
    chunk = rows // 8
    return pl.pallas_call(
        scatter_kernel,
        grid=(8,),
        out_shape=jax.ShapeDtypeStruct((rows, width), F32),
        in_specs=[smem, pl.BlockSpec((chunk, width), lambda i: (i, 0))],
        out_specs=pl.BlockSpec((rows, width), lambda i: (0, 0)),
        compiler_params=pltpu.CompilerParams(vmem_limit_bytes=16 * 1024 * 1024),
        name="hss_scatter",
    )(order, y)


def solution(mesh):
    in_specs = (
        P(None, ("top", "sub")),
        P(("top", "sub"), None),
        P(("top", "sub"), None),
        P(("top", "sub"), None),
        P(("top", "sub"), None, None),
        P(("top", "sub"), None, None),
        P("top", None, None, None),
        P("top", None, None, None),
        P(),
        P(),
    )
    out_specs = P(("top", "sub"), None)
    body = functools.partial(local, mesh.shape["sub"], mesh.shape["top"])
    return jax.shard_map(
        body, mesh=mesh, in_specs=in_specs, out_specs=out_specs, check_vma=False
    )
```

time: 146 us -> 63.7 us (0.44)
  the two profiles are of different devices: /device:TPU:4 before, /device:TPU:1 now
where the time goes in v1:
time: 63.7 us; the launch traced here: 63.2 us
  Pallas kernels  52.5 us (82%)
  local copies, waits for them, and re-layouts  10.7 us (17%)
    pallas_call x1, Pallas kernels, local(): pl.pallas_call(functools.partial(main_kernel, n_sub, n_top), out_shape=ja...  45.7 us
    unnamed x20, local copies, waits for them, and re-layouts  10.7 us
    pallas_call x1, Pallas kernels, local(): pl.pallas_call(scatter_kernel, grid=(8,), out_shape=jax.ShapeDtypeStruct(...  6.73 us

profile of v1, /device:TPU:1, one launch (start us, length us, event | category | flops | bytes accessed | tf_op | source)
XLA Modules:
  0.0 63.2 jit_solution(13192666017707102721)
XLA Ops:
  0.0 0.0 copy-start.1
  0.0 1.6 %copy-done.1 = bf16[1,62,128,128]{3,2,1,0:T(8,128)(2,1)S(1)} copy-done((bf16[1,62,128,128]{3,2,1,0:T(8,128)(2,1)S(1)}, bf16[1,62,128,128]{3,2,1,0:T(8,128)(2,1)}, u32[]{:S(2)}) %copy-start.1) | copy-done | bytes 2031640
  1.6 0.0 copy-start.2
  1.6 1.2 %copy-done.2 = bf16[4096,128]{1,0:T(8,128)(2,1)S(1)} copy-done((bf16[4096,128]{1,0:T(8,128)(2,1)S(1)}, bf16[4096,128]{1,0:T(8,128)(2,1)}, u32[]{:S(2)}) %copy-start.2) | copy-done | bytes 1048600
  2.8 0.0 copy-start.3
  2.8 1.2 %copy-done.3 = bf16[1,31,128,128]{3,2,1,0:T(8,128)(2,1)S(1)} copy-done((bf16[1,31,128,128]{3,2,1,0:T(8,128)(2,1)S(1)}, bf16[1,31,128,128]{3,2,1,0:T(8,128)(2,1)}, u32[]{:S(2)}) %copy-start.3) | copy-done | bytes 1015832
  4.0 0.0 copy-start.4
  4.0 1.0 %copy-done.4 = bf16[12,128,128]{2,1,0:T(8,128)(2,1)S(1)} copy-done((bf16[12,128,128]{2,1,0:T(8,128)(2,1)S(1)}, bf16[12,128,128]{2,1,0:T(8,128)(2,1)}, u32[]{:S(2)}) %copy-start.4) | copy-done | bytes 393240
  5.0 0.0 copy-start.5
  5.0 0.9 %copy-done.5 = bf16[7,128,128]{2,1,0:T(8,128)(2,1)S(1)} copy-done((bf16[7,128,128]{2,1,0:T(8,128)(2,1)S(1)}, bf16[7,128,128]{2,1,0:T(8,128)(2,1)}, u32[]{:S(2)}) %copy-start.5) | copy-done | bytes 229400
  5.9 0.0 copy-start.6
  5.9 0.8 %copy-done.6 = f32[3,4096]{1,0:T(4,128)S(1)} copy-done((f32[3,4096]{1,0:T(4,128)S(1)}, f32[3,4096]{1,0:T(4,128)}, u32[]{:S(2)}) %copy-start.6) | copy-done | bytes 49176
  6.8 0.0 copy-start.7
  6.8 0.8 %copy-done.7 = bf16[2,128,128]{2,1,0:T(8,128)(2,1)S(1)} copy-done((bf16[2,128,128]{2,1,0:T(8,128)(2,1)S(1)}, bf16[2,128,128]{2,1,0:T(8,128)(2,1)}, u32[]{:S(2)}) %copy-start.7) | copy-done | bytes 65560
  7.6 0.0 copy-start.8
  7.6 0.7 %copy-done.8 = s32[1,4096]{1,0:T(1,128)S(1)} copy-done((s32[1,4096]{1,0:T(1,128)S(1)}, s32[1,4096]{1,0:T(1,128)}, u32[]{:S(2)}) %copy-start.8) | copy-done | bytes 16408
  8.3 0.0 copy-start.9
  8.3 0.8 %copy-done.9 = bf16[1,128,128]{2,1,0:T(8,128)(2,1)S(1)} copy-done((bf16[1,128,128]{2,1,0:T(8,128)(2,1)S(1)}, bf16[1,128,128]{2,1,0:T(8,128)(2,1)}, u32[]{:S(2)}) %copy-start.9) | copy-done | bytes 32792
  9.1 45.7 %hss_main.1.y_ref = f32[4096,128]{1,0:T(8,128)} custom-call(s32[1,4096]{1,0:T(1,128)S(1)} %copy-done.8, f32[3,4096]{1,0:T(4,128)S(1)} %copy-done.6, f32[4096,128]{1,0:T(8,128)} %vectors_hbm.1, bf16[4096,128]{1,0:T(8,128)(2,1)S(1)} %copy-done.2, bf16[2,128,128]{2,1,0:T(8,128)(2,1)S(1)} %copy-done.7, bf16[1,128,128]{2,1,0:T(8,128)(2,1)S(1)} %copy-done.9, ...), custom_call_target="tpu_custom_call" | custom-call | tf_op jit(solution)/shard_map/hss_main/pallas_call | solution.py:430
  54.9 0.0 copy-start
  54.9 1.6 %copy-done = f32[4096,128]{1,0:T(8,128)S(1)} copy-done((f32[4096,128]{1,0:T(8,128)S(1)}, f32[4096,128]{1,0:T(8,128)}, u32[]{:S(2)}) %copy-start) | copy-done | bytes 2097176
  56.4 6.7 %hss_scatter.1 = f32[4096,128]{1,0:T(8,128)} custom-call(s32[1,4096]{1,0:T(1,128)S(1)} %copy-done.8, f32[4096,128]{1,0:T(8,128)S(1)} %copy-done), custom_call_target="tpu_custom_call" | custom-call | tf_op jit(solution)/shard_map/hss_scatter/pallas_call | solution.py:453
Async XLA Ops:
  0.0 1.6 %copy-start.1 = (bf16[1,62,128,128]{3,2,1,0:T(8,128)(2,1)S(1)}, bf16[1,62,128,128]{3,2,1,0:T(8,128)(2,1)}, u32[]{:S(2)}) copy-start(bf16[1,62,128,128]{3,2,1,0:T(8,128)(2,1)} %param.16) | copy-start | bytes 6094852
  1.6 1.2 %copy-start.2 = (bf16[4096,128]{1,0:T(8,128)(2,1)S(1)}, bf16[4096,128]{1,0:T(8,128)(2,1)}, u32[]{:S(2)}) copy-start(bf16[4096,128]{1,0:T(8,128)(2,1)} %gen_hbm.1) | copy-start | bytes 3145732
  2.8 1.2 %copy-start.3 = (bf16[1,31,128,128]{3,2,1,0:T(8,128)(2,1)S(1)}, bf16[1,31,128,128]{3,2,1,0:T(8,128)(2,1)}, u32[]{:S(2)}) copy-start(bf16[1,31,128,128]{3,2,1,0:T(8,128)(2,1)} %param.17) | copy-start | bytes 3047428
  4.0 1.0 %copy-start.4 = (bf16[12,128,128]{2,1,0:T(8,128)(2,1)S(1)}, bf16[12,128,128]{2,1,0:T(8,128)(2,1)}, u32[]{:S(2)}) copy-start(bf16[12,128,128]{2,1,0:T(8,128)(2,1)} %top_w_hbm.1) | copy-start | bytes 1179652
  5.0 0.9 %copy-start.5 = (bf16[7,128,128]{2,1,0:T(8,128)(2,1)S(1)}, bf16[7,128,128]{2,1,0:T(8,128)(2,1)}, u32[]{:S(2)}) copy-start(bf16[7,128,128]{2,1,0:T(8,128)(2,1)} %top_b_hbm.1) | copy-start | bytes 688132
  5.9 0.8 %copy-start.6 = (f32[3,4096]{1,0:T(4,128)S(1)}, f32[3,4096]{1,0:T(4,128)}, u32[]{:S(2)}) copy-start(f32[3,4096]{1,0:T(4,128)} %coords_ref.1) | copy-start | bytes 147460
  6.8 0.8 %copy-start.7 = (bf16[2,128,128]{2,1,0:T(8,128)(2,1)S(1)}, bf16[2,128,128]{2,1,0:T(8,128)(2,1)}, u32[]{:S(2)}) copy-start(bf16[2,128,128]{2,1,0:T(8,128)(2,1)} %leaf_w_hbm.1) | copy-start | bytes 196612
  7.6 0.7 %copy-start.8 = (s32[1,4096]{1,0:T(1,128)S(1)}, s32[1,4096]{1,0:T(1,128)}, u32[]{:S(2)}) copy-start(s32[1,4096]{1,0:T(1,128)} %order_ref.3) | copy-start | bytes 49156
  8.3 0.8 %copy-start.9 = (bf16[1,128,128]{2,1,0:T(8,128)(2,1)S(1)}, bf16[1,128,128]{2,1,0:T(8,128)(2,1)}, u32[]{:S(2)}) copy-start(bf16[1,128,128]{2,1,0:T(8,128)(2,1)} %leaf_b_hbm.1) | copy-start | bytes 98308
  54.9 1.6 %copy-start = (f32[4096,128]{1,0:T(8,128)S(1)}, f32[4096,128]{1,0:T(8,128)}, u32[]{:S(2)}) copy-start(f32[4096,128]{1,0:T(8,128)} %hss_main.1.y_ref) | copy-start | bytes 6291460

commit v2 on v1

v2 whole, which is shorter than its diff:
```python
import functools

import jax
import jax.numpy as jnp
from jax import lax
from jax.experimental import pallas as pl
from jax.experimental.pallas import tpu as pltpu
from jax.sharding import PartitionSpec as P

NUGGET = 0.1
DECAY_RATE = 3.0**0.5 / 0.004
TINY = 1e-30
VMEM_LIMIT = 63 * 1024 * 1024
BLOCK = 256
BLOCKS = 8
WIDE = 5 * BLOCK
NARROW = 4 * BLOCK
F32 = jnp.float32
BF16 = jnp.bfloat16
NN = (((1,), (0,)), ((), ()))
NT = (((1,), (1,)), ((), ()))


def pieces(x):
    high = x.astype(BF16)
    low = (x - high.astype(F32)).astype(BF16)
    return jnp.concatenate([high, low], axis=0)


def product(x, matrix, form):
    rows = x.shape[0]
    both = lax.dot_general(pieces(x), matrix, form, preferred_element_type=F32)
    return both[:rows] + both[rows:]


def place_kernel(order_ref, out_ref):
    rows = order_ref.shape[1]
    value = order_ref[...]
    high = value // 128
    low = value - high * 128
    position = lax.broadcasted_iota(jnp.int32, (1, rows), 1)
    pos_high = position // 64
    pos_low = position - pos_high * 64
    at_high = lax.broadcasted_iota(jnp.int32, (rows // 128, rows), 0) == high
    at_low = lax.broadcasted_iota(jnp.int32, (128, rows), 0) == low
    digits = jnp.concatenate(
        [
            jnp.where(at_high, pos_high.astype(F32), 0.0),
            jnp.where(at_high, pos_low.astype(F32), 0.0),
        ],
        axis=0,
    ).astype(BF16)
    found = lax.dot_general(
        digits, jnp.where(at_low, 1.0, 0.0).astype(BF16), NT, preferred_element_type=F32
    )
    half = rows // 128
    place = (found[:half] * 64.0 + found[half:]).astype(jnp.int32)
    out_ref[...] = jnp.clip(place, 0, rows - 1)


def main_kernel(
    n_sub,
    n_top,
    order,
    inverse,
    table_hbm,
    coords_hbm,
    vectors_hbm,
    gen_hbm,
    leaf_w_hbm,
    leaf_b_hbm,
    sub_w_hbm,
    sub_b_hbm,
    top_w_hbm,
    top_b_hbm,
    near_hbm,
    ucat_hbm,
    fcat_hbm,
    coords,
    vec,
    ordered,
    v_ext,
    v_t,
    gen,
    leaf_w,
    leaf_b,
    sub_w,
    sub_b,
    top_w,
    top_b,
    x_rows,
    x_cols,
    k_0,
    k_1,
    k_2,
    k_3,
    k_4,
    y_row,
    y_col,
    y_all,
    near,
    u_wide,
    u_moved,
    ucat,
    fcat,
    table,
    send_c,
    coef,
    sib,
    field,
    back,
    top_c,
    dev_f,
    g_leaf,
    in_sem,
    out_sem,
    send_sem,
    recv_sem,
):
    k_bufs = [k_0, k_1, k_2, k_3, k_4]
    leaf = v_t.shape[2]
    rows = vec.shape[0]
    width = vec.shape[1]
    share = width // n_sub
    extra = v_ext.shape[1] - leaf
    me_sub = lax.axis_index("sub")
    me_top = lax.axis_index("top")

    barrier = pltpu.get_barrier_semaphore()

    def load(i, source, target):
        copy = pltpu.make_async_copy(source, target, in_sem.at[i])
        copy.start()
        return copy

    load_coords = load(0, coords_hbm, coords)
    load_table = load(1, table_hbm, table)
    quarter = rows // 4
    load_vec = [
        load(3 + i, vectors_hbm.at[pl.ds(i * quarter, quarter)], vec.at[pl.ds(i * quarter, quarter)])
        for i in range(4)
    ]
    load_leaf = [
        load(7, gen_hbm, gen),
        load(8, leaf_w_hbm, leaf_w),
        load(9, leaf_b_hbm, leaf_b),
    ]
    load_sub = [load(10, sub_w_hbm, sub_w), load(11, sub_b_hbm, sub_b)]
    load_top = [load(12, top_w_hbm, top_w), load(13, top_b_hbm, top_b)]

    def greet(axis, count, place):
        def one(k, _):
            pl.semaphore_signal(
                barrier,
                inc=1,
                device_id={axis: lax.rem(place + k, count)},
                device_id_type=pl.DeviceIdType.MESH,
            )
            return 0

        lax.fori_loop(1, count, one, 0)

    greet("sub", n_sub, me_sub)
    greet("top", n_top, me_top)

    def spread(start):
        for axis in range(3):
            row = coords[axis : axis + 1, pl.ds(start, 128)] * DECAY_RATE
            x_rows[axis, pl.ds(start, 128), :] = jnp.broadcast_to(row, (128, 128)).T

    def spread_block(at, block):
        spread(at * leaf + block * BLOCK)
        spread(at * leaf + block * BLOCK + 128)

    load_coords.wait()
    spread_block(0, 0)
    spread_block(1, 0)
    for at in range(2):
        for axis in range(3):
            row = coords[axis : axis + 1, at * leaf : (at + 1) * leaf] * DECAY_RATE
            whole = jnp.broadcast_to(row, (8, leaf))
            x_cols[axis, at, :, :leaf] = whole
            x_cols[axis, at, :, leaf:] = whole[:, :extra]
    y_col[...] = jnp.zeros_like(y_col)

    strips = [(at, block) for block in range(BLOCKS) for at in range(2)]

    def size_of(index):
        return WIDE if strips[index][1] < BLOCKS // 2 else NARROW

    def evaluate(index, first, low, high):
        at, block = strips[index]
        size = high - low
        here = pl.ds(pl.multiple_of(at * leaf + block * BLOCK + first, 16), 16)
        there = pl.ds(block * BLOCK + low, size)
        total = None
        for axis in range(3):
            x_i = jnp.concatenate([x_rows[axis, here, :]] * (size // 128), axis=1)
            x_j = x_cols[axis, at, :, there]
            offset = x_i - jnp.concatenate([x_j, x_j], axis=0)
            square = offset * offset
            total = square + TINY if total is None else total + square
        scaled = total * lax.rsqrt(total)
        value = (1.0 + scaled) * jnp.exp(-scaled)
        k_bufs[index % 5][pl.ds(pl.multiple_of(first, 16), 16), pl.ds(low, size)] = value.astype(BF16)

    def apply(index):
        at, block = strips[index]
        size = size_of(index)
        held = k_bufs[index % 5]
        start = block * BLOCK
        y_row[at, pl.ds(start, BLOCK), :] = jnp.dot(
            held[:, :size], v_ext[at, pl.ds(start, size), :], preferred_element_type=F32
        )
        y_col[at, :, pl.ds(start + BLOCK, size - BLOCK)] += jnp.dot(
            v_t[at, :, pl.ds(start, BLOCK)], held[:, BLOCK:size], preferred_element_type=F32
        )

    for copy in load_vec:
        copy.wait()

    def turn(start):
        at = start // leaf
        inside = pl.multiple_of(start - at * leaf, 128)
        some = ordered[pl.ds(start, 128), :]
        v_ext[at, pl.ds(inside, 128), :] = some.astype(BF16)
        v_t[at, :, pl.ds(inside, 128)] = some.T.astype(BF16)

    def first_strip(index):
        def part(p, _):
            start = pl.multiple_of(index * 1024 + p * 128, 128)
            for group in range(4):
                begin = start + group * 32
                held = [vec[pl.ds(order[0, begin + k], 1), :] for k in range(32)]
                low = (group % 2) * (WIDE // 2)
                evaluate(index, p * 32 + (group // 2) * 16, low, low + WIDE // 2)
                for k in range(32):
                    ordered[pl.ds(begin + k, 1), :] = held[k]
            turn(pl.multiple_of(jnp.maximum(start - 128, 0), 128))
            if index == 0:
                spread(
                    pl.multiple_of(
                        lax.rem(p // 2, 2) * leaf + (1 + p // 4) * BLOCK + lax.rem(p, 2) * 128, 128
                    )
                )
            return 0

        lax.fori_loop(0, 8, part, 0, unroll=True)

    for index in range(4):
        first_strip(index)
    turn(rows - 128)
    for at in range(2):
        v_ext[at, leaf:, :] = v_ext[at, :extra, :]

    for copy in load_leaf:
        copy.wait()
    left = jnp.dot(v_t[0], gen[:leaf, :], preferred_element_type=F32)
    right = jnp.dot(v_t[1], gen[leaf:, :], preferred_element_type=F32)
    device_c = product(left, leaf_w[0], NN) + product(right, leaf_w[1], NN)
    for r in range(n_sub):
        send_c[r] = device_c[r * share : (r + 1) * share, :]
    pl.semaphore_wait(barrier, n_sub + n_top - 2)

    def sub_partners():
        inner = 4 if n_sub % 4 == 0 else 1
        outer = n_sub // inner

        def distance(k):
            step, turn = k // inner, k % inner
            return min(step, outer - step) + min(turn, inner - turn)

        for k in sorted(range(1, n_sub), key=lambda k: -distance(k)):
            step, turn = k // inner, k % inner
            yield (
                lax.rem(me_sub // inner + step, outer) * inner
                + lax.rem(lax.rem(me_sub, inner) + turn, inner)
            )

    def top_partners():
        for k in sorted(range(1, n_top), key=lambda k: -min(k, n_top - k)):
            yield lax.rem(me_top + k, n_top)

    def exchange(axis, count, place, partners, stage, source, target, base):
        def copy(partner, slot):
            return pltpu.make_async_remote_copy(
                src_ref=source(partner),
                dst_ref=target.at[base + slot],
                send_sem=send_sem.at[stage, partner],
                recv_sem=recv_sem.at[stage, slot],
                device_id={axis: partner},
                device_id_type=pl.DeviceIdType.MESH,
            )

        def start():
            for partner in partners():
                copy(partner, place).start()

        def finish_send(k, _):
            copy(lax.rem(place + k, count), place).wait_send()
            return 0

        def finish_recv(k, _):
            partner = lax.rem(place + k, count)
            copy(partner, partner).wait_recv()
            return 0

        return (
            start,
            lambda: lax.fori_loop(1, count, finish_send, 0),
            lambda: lax.fori_loop(1, count, finish_recv, 0),
        )

    up_start, up_sent, up_here = exchange(
        "sub", n_sub, me_sub, sub_partners, 0, lambda partner: send_c.at[partner], coef, n_sub
    )
    up_start()
    coef[n_sub + me_sub] = send_c[me_sub]
    g_leaf[0] = product(right, leaf_b[0], NT)
    g_leaf[1] = product(left, leaf_b[0], NN)

    u_wide[...] = gen[...].astype(F32)
    load_table.wait()

    def work(index, ready, moving):
        at, block = strips[index]
        for done in ready:
            apply(done)

        size = size_of(index)

        def part(p, _):
            if not moving:
                evaluate(index, p * 16, 0, size)
                return 0
            line = (index - 4) * 4 + p // 4
            begin = lax.rem(p, 4) * 32
            start = pl.multiple_of((index - 4) * 512 + p * 32, 32)
            held = [u_wide[pl.ds(inverse[line, begin + k], 1), :] for k in range(32)]
            evaluate(index, p * 16, 0, size)
            for k in range(32):
                u_moved[pl.ds(start + k, 1), :] = held[k]
            return 0

        lax.fori_loop(0, 16, part, 0, unroll=True)
        if moving:
            for line in range((index - 4) * 4, (index - 3) * 4):
                here = slice(line * 128, (line + 1) * 128)
                second = jnp.where(table[line : line + 1, :] >= leaf, 1.0, 0.0)
                second = jnp.broadcast_to(second, (128, 128)).T > 0.5
                some = u_moved[here, :]
                ucat[here, :width] = jnp.where(second, 0.0, some).astype(BF16)
                ucat[here, width:] = jnp.where(second, some, 0.0).astype(BF16)
        if block + 1 < BLOCKS and block >= 2:
            spread_block(at, block + 1)

    work(4, [0, 1], True)
    work(5, [2], True)
    work(6, [3, 4], True)
    work(7, [5], True)
    work(8, [6, 7], True)
    work(9, [8], True)

    for copy in load_sub:
        copy.wait()
    up_here()

    def upward(held, matrices, parent, offset):
        pair = jnp.concatenate([held[2 * parent], held[2 * parent + 1]], axis=1)
        both = matrices[pl.ds(2 * parent - offset, 2)].reshape(2 * width, width)
        held[parent] = product(pair, both, NN)

    count = n_sub // 2
    while count >= 1:
        lax.fori_loop(
            count, 2 * count, lambda p, _: (upward(coef, sub_w, p, 2), 0)[1], 0, unroll=True
        )
        count //= 2
    top_start, top_sent, top_here = exchange(
        "top", n_top, me_top, top_partners, 1, lambda partner: coef.at[1], top_c, n_top
    )
    top_start()
    top_c[n_top + me_top] = coef[1]

    def siblings(parent, _):
        matrix = sub_b[parent - 1]
        sib[2 * parent] = product(coef[2 * parent + 1], matrix, NT)
        sib[2 * parent + 1] = product(coef[2 * parent], matrix, NN)
        return 0

    lax.fori_loop(1, n_sub, siblings, 0, unroll=True)

    work(10, [9], True)
    work(11, [10], True)
    u_write = pltpu.make_async_copy(ucat, ucat_hbm, out_sem.at[0])
    u_write.start()
    work(12, [11], False)
    work(13, [12], False)

    for copy in load_top:
        copy.wait()
    top_here()
    count = n_top // 2
    while count >= 2:
        lax.fori_loop(
            count, 2 * count, lambda p, _: (upward(top_c, top_w, p, 4), 0)[1], 0, unroll=True
        )
        count //= 2
    now = None
    count = 2
    while count <= n_top:
        node = count + me_top // (n_top // count)
        parent = node // 2
        is_left = node - 2 * parent == 0
        other = jnp.where(is_left, node + 1, node - 1)
        matrix = top_b[parent - 1]
        incoming = jnp.where(
            is_left, product(top_c[other], matrix, NT), product(top_c[other], matrix, NN)
        )
        now = incoming if now is None else product(now, top_w[node - 4], NT) + incoming
        count *= 2
    field[1] = now

    def downward(parent, _):
        both = sub_w[pl.ds(2 * parent - 2, 2)].reshape(2 * width, width)
        down = product(field[parent], both, NT)
        field[2 * parent] = down[:, :width] + sib[2 * parent]
        field[2 * parent + 1] = down[:, width:] + sib[2 * parent + 1]
        return 0

    count = 1
    while count < n_sub:
        lax.fori_loop(count, 2 * count, downward, 0, unroll=True)
        count *= 2
    down_start, down_sent, down_here = exchange(
        "sub", n_sub, me_sub, sub_partners, 2, lambda partner: field.at[n_sub + partner], back, 0
    )
    down_start()
    back[me_sub] = field[n_sub + me_sub]

    work(14, [13], False)
    work(15, [14], False)
    apply(15)
    for at in range(2):
        for block in range(BLOCKS):
            start = at * leaf + block * BLOCK
            here = slice(block * BLOCK, (block + 1) * BLOCK)
            turned = y_col[at, :, here]
            if (block + 1) * BLOCK <= extra:
                turned = turned + y_col[at, :, leaf + block * BLOCK : leaf + (block + 1) * BLOCK]
            y_all[start : start + BLOCK, :] = (
                y_row[at, here, :] + turned.T + NUGGET * ordered[start : start + BLOCK, :]
            )

    def move_back(line, _):
        start = pl.multiple_of(line * 128, 128)

        def move(k, _):
            near[pl.ds(start + k, 1), :] = y_all[pl.ds(inverse[line, k], 1), :]
            return 0

        lax.fori_loop(0, 128, move, 0, unroll=True)
        return 0

    writes = [u_write]
    for i in range(4):
        lax.fori_loop(i * rows // 512, (i + 1) * rows // 512, move_back, 0, unroll=True)
        some = pl.ds(i * quarter, quarter)
        write = pltpu.make_async_copy(near.at[some], near_hbm.at[some], out_sem.at[1 + i])
        write.start()
        writes.append(write)

    down_here()
    for r in range(n_sub):
        dev_f[r * share : (r + 1) * share, :] = back[r]
    device_f = dev_f[...]
    for at in range(2):
        fcat[:, at * width : (at + 1) * width] = (
            product(device_f, leaf_w[at], NT) + g_leaf[at]
        ).astype(BF16)
    f_write = pltpu.make_async_copy(fcat, fcat_hbm, out_sem.at[5])
    f_write.start()
    writes.append(f_write)
    up_sent()
    top_sent()
    down_sent()
    for write in writes:
        write.wait()


def far_kernel(near_ref, ucat_ref, fcat_ref, out_ref):
    out_ref[...] = near_ref[...] + lax.dot_general(
        ucat_ref[...], fcat_ref[...], NT, preferred_element_type=F32
    )


def local(
    n_sub,
    n_top,
    coords,
    vectors,
    order,
    generators,
    leaf_transfer,
    leaf_coupling,
    sub_transfer,
    sub_coupling,
    top_transfer,
    top_coupling,
):
    rows, width = vectors.shape
    leaf = rows // 2
    rank = generators.shape[1]
    share = width // n_sub
    extended = leaf + 3 * BLOCK
    hbm = pl.BlockSpec(memory_space=pl.ANY)
    smem = pl.BlockSpec(memory_space=pltpu.SMEM)
    inverse = pl.pallas_call(
        place_kernel,
        out_shape=jax.ShapeDtypeStruct((rows // 128, 128), jnp.int32),
        compiler_params=pltpu.CompilerParams(vmem_limit_bytes=VMEM_LIMIT),
        name="hss_place",
    )(order)
    scratch = [
        pltpu.VMEM((3, rows), F32),
        pltpu.VMEM((rows, width), F32),
        pltpu.VMEM((rows, width), F32),
        pltpu.VMEM((2, extended, width), BF16),
        pltpu.VMEM((2, width, leaf), BF16),
        pltpu.VMEM((rows, rank), BF16),
        pltpu.VMEM(leaf_transfer.shape, BF16),
        pltpu.VMEM(leaf_coupling.shape, BF16),
        pltpu.VMEM(sub_transfer.shape[1:], BF16),
        pltpu.VMEM(sub_coupling.shape[1:], BF16),
        pltpu.VMEM(top_transfer.shape, BF16),
        pltpu.VMEM(top_coupling.shape, BF16),
        pltpu.VMEM((3, rows, 128), F32),
        pltpu.VMEM((3, 2, 8, extended), F32),
        *[pltpu.VMEM((BLOCK, WIDE), BF16) for _ in range(5)],
        pltpu.VMEM((2, leaf, width), F32),
        pltpu.VMEM((2, width, extended), F32),
        pltpu.VMEM((rows, width), F32),
        pltpu.VMEM((rows, width), F32),
        pltpu.VMEM((rows, rank), F32),
        pltpu.VMEM((rows, rank), F32),
        pltpu.VMEM((rows, 2 * rank), BF16),
        pltpu.VMEM((width, 2 * rank), BF16),
        pltpu.VMEM((rows // 128, 128), jnp.int32),
        pltpu.VMEM((n_sub, share, rank), F32),
        pltpu.VMEM((2 * n_sub, share, rank), F32),
        pltpu.VMEM((2 * n_sub, share, rank), F32),
        pltpu.VMEM((2 * n_sub, share, rank), F32),
        pltpu.VMEM((n_sub, share, rank), F32),
        pltpu.VMEM((2 * n_top, share, rank), F32),
        pltpu.VMEM((width, rank), F32),
        pltpu.VMEM((2, width, rank), F32),
        pltpu.SemaphoreType.DMA((14,)),
        pltpu.SemaphoreType.DMA((6,)),
        pltpu.SemaphoreType.DMA((3, max(n_sub, n_top))),
        pltpu.SemaphoreType.DMA((3, max(n_sub, n_top))),
    ]
    near, ucat, fcat = pl.pallas_call(
        functools.partial(main_kernel, n_sub, n_top),
        out_shape=(
            jax.ShapeDtypeStruct((rows, width), F32),
            jax.ShapeDtypeStruct((rows, 2 * rank), BF16),
            jax.ShapeDtypeStruct((width, 2 * rank), BF16),
        ),
        in_specs=[smem, smem] + [hbm] * 10,
        out_specs=(hbm, hbm, hbm),
        scratch_shapes=scratch,
        compiler_params=pltpu.CompilerParams(
            collective_id=0, has_side_effects=True, vmem_limit_bytes=VMEM_LIMIT
        ),
        name="hss_main",
    )(
        order,
        inverse,
        inverse,
        coords,
        vectors,
        generators,
        leaf_transfer,
        leaf_coupling,
        sub_transfer[0],
        sub_coupling[0],
        top_transfer,
        top_coupling,
    )
    chunk = rows // 2
    return pl.pallas_call(
        far_kernel,
        grid=(2,),
        out_shape=jax.ShapeDtypeStruct((rows, width), F32),
        in_specs=[
            pl.BlockSpec((chunk, width), lambda i: (i, 0)),
            pl.BlockSpec((chunk, 2 * rank), lambda i: (i, 0)),
            pl.BlockSpec((width, 2 * rank), lambda i: (0, 0)),
        ],
        out_specs=pl.BlockSpec((chunk, width), lambda i: (i, 0)),
        compiler_params=pltpu.CompilerParams(vmem_limit_bytes=VMEM_LIMIT),
        name="hss_far",
    )(near, ucat, fcat)


def solution(mesh):
    in_specs = (
        P(None, ("top", "sub")),
        P(("top", "sub"), None),
        P(("top", "sub"), None),
        P(("top", "sub"), None),
        P(("top", "sub"), None, None),
        P(("top", "sub"), None, None),
        P("top", None, None, None),
        P("top", None, None, None),
        P(),
        P(),
    )
    out_specs = P(("top", "sub"), None)
    body = functools.partial(local, mesh.shape["sub"], mesh.shape["top"])
    return jax.shard_map(
        body, mesh=mesh, in_specs=in_specs, out_specs=out_specs, check_vma=False
    )
```

time: 63.7 us -> 45 us (0.71)
  local copies, waits for them, and re-layouts: 10.7 us -> 0 us
  Pallas kernels: 52.5 us -> 44.7 us
    unnamed x20 -> x0, local copies, waits for them, and re-layouts: 10.7 us -> none
    pallas_call x2 -> x3, Pallas kernels: 52.5 us -> 44.7 us  [the longest x1 39.2 us: local(): pl.pallas_call(functools.partial(main_kernel, n_sub, n_top), out_shape=(j...]
where the time goes in v2:
time: 45 us; the launch traced here: 44.7 us
  Pallas kernels  44.7 us (99%)
    pallas_call x1, Pallas kernels, local(): pl.pallas_call(functools.partial(main_kernel, n_sub, n_top), out_shape=(j...  39.2 us
    pallas_call x1, Pallas kernels, local(): pl.pallas_call(far_kernel, grid=(2,), out_shape=jax.ShapeDtypeStruct((row...  3.61 us
    pallas_call x1, Pallas kernels, local(): pl.pallas_call(place_kernel, out_shape=jax.ShapeDtypeStruct((rows // 128,...  1.82 us

profile of v2, /device:TPU:1, one launch (start us, length us, event | category | flops | bytes accessed | tf_op | source)
XLA Modules:
  0.0 44.7 jit_solution(12719742870884734770)
XLA Ops:
  0.0 1.8 %hss_place.1.inverse.table_hbm = s32[32,128]{1,0:T(8,128)} custom-call(s32[1,4096]{1,0:T(1,128)} %order.1), custom_call_target="tpu_custom_call" | custom-call | tf_op jit(solution)/shard_map/hss_place/pallas_call | solution.py:518
  1.8 39.2 %hss_main.1 = (f32[4096,128]{1,0:T(8,128)}, bf16[4096,256]{1,0:T(8,128)(2,1)}, bf16[128,256]{1,0:T(8,128)(2,1)}) custom-call(s32[1,4096]{1,0:T(1,128)} %order.1, s32[32,128]{1,0:T(8,128)} %hss_place.1.inverse.table_hbm, s32[32,128]{1,0:T(8,128)} %hss_place.1.inverse.table_hbm, f32[3,4096]{1,0:T(4,128)} %coords_hbm.1, f32[4096,128]{1,0:T(8,128)} %vectors_hbm.1, ...), custom_call_target="tpu_custom_call" | custom-call | tf_op jit(solution)/shard_map/hss_main/pallas_call | solution.py:562
  41.1 3.6 %hss_far.1 = f32[4096,128]{1,0:T(8,128)} custom-call(f32[4096,128]{1,0:T(8,128)} %get-tuple-element.8.near_ref, bf16[4096,256]{1,0:T(8,128)(2,1)} %get-tuple-element.9.ucat_ref, bf16[128,256]{1,0:T(8,128)(2,1)} %get-tuple-element.10.fcat_ref), custom_call_target="tpu_custom_call" | custom-call | tf_op jit(solution)/shard_map/hss_far/pallas_call | solution.py:591

commit v3 on v2

--- a/solution.py
+++ b/solution.py
@@ -395,7 +395,6 @@
     u_write = pltpu.make_async_copy(ucat, ucat_hbm, out_sem.at[0])
     u_write.start()
     work(12, [11], False)
-    work(13, [12], False)
 
     for copy in load_top:
         copy.wait()
@@ -438,6 +437,7 @@
     down_start()
     back[me_sub] = field[n_sub + me_sub]
 
+    work(13, [12], False)
     work(14, [13], False)
     work(15, [14], False)
     apply(15)

time: 45 us -> 45 us (level)
  no operation moved by 1% of the time
where the time goes in v3:
time: 45 us; the launch traced here: 44.6 us
  Pallas kernels  44.6 us (99%)
    pallas_call x1, Pallas kernels, local(): pl.pallas_call(functools.partial(main_kernel, n_sub, n_top), out_shape=(j...  39.2 us
    pallas_call x1, Pallas kernels, local(): pl.pallas_call(far_kernel, grid=(2,), out_shape=jax.ShapeDtypeStruct((row...  3.62 us
    pallas_call x1, Pallas kernels, local(): pl.pallas_call(place_kernel, out_shape=jax.ShapeDtypeStruct((rows // 128,...  1.82 us

profile of v3, /device:TPU:1, one launch (start us, length us, event | category | flops | bytes accessed | tf_op | source)
XLA Modules:
  0.0 44.6 jit_solution(11820834501651346188)
XLA Ops:
  0.0 1.8 %hss_place.1.inverse.table_hbm = s32[32,128]{1,0:T(8,128)} custom-call(s32[1,4096]{1,0:T(1,128)} %order.1), custom_call_target="tpu_custom_call" | custom-call | tf_op jit(solution)/shard_map/hss_place/pallas_call | solution.py:518
  1.8 39.2 %hss_main.1 = (f32[4096,128]{1,0:T(8,128)}, bf16[4096,256]{1,0:T(8,128)(2,1)}, bf16[128,256]{1,0:T(8,128)(2,1)}) custom-call(s32[1,4096]{1,0:T(1,128)} %order.1, s32[32,128]{1,0:T(8,128)} %hss_place.1.inverse.table_hbm, s32[32,128]{1,0:T(8,128)} %hss_place.1.inverse.table_hbm, f32[3,4096]{1,0:T(4,128)} %coords_hbm.1, f32[4096,128]{1,0:T(8,128)} %vectors_hbm.1, ...), custom_call_target="tpu_custom_call" | custom-call | tf_op jit(solution)/shard_map/hss_main/pallas_call | solution.py:562
  41.0 3.6 %hss_far.1 = f32[4096,128]{1,0:T(8,128)} custom-call(f32[4096,128]{1,0:T(8,128)} %get-tuple-element.8.near_ref, bf16[4096,256]{1,0:T(8,128)(2,1)} %get-tuple-element.9.ucat_ref, bf16[128,256]{1,0:T(8,128)(2,1)} %get-tuple-element.10.fcat_ref), custom_call_target="tpu_custom_call" | custom-call | tf_op jit(solution)/shard_map/hss_far/pallas_call | solution.py:591
